TPU v7x, 256 devices: a whole 4x4x8 slice. The times are simulated.
256 devices in a mesh: replica: 8 (over y, z_hi), fsdp: 32 (over x, z_lo, core).
Axes of the slice: x: 4, y: 4, z: 8 (z_hi: 2, z_lo: 4; z = z_hi * 4 + z_lo), core: 2. Of those that a mesh axis runs over, the one named last changes fastest.
Arguments:
- activations: bfloat16 [8, 4096, 8192], P('replica', 'fsdp'), may hold values from -6 to 6
- cotangent: bfloat16 [8, 4096, 1024], P('replica', 'fsdp'), may hold values from -12 to 12
- weight: float32 [8, 8192, 1024], P('replica', 'fsdp'), may hold values from -6 to 6
- moment: float32 [8, 8192, 1024], P('replica', 'fsdp'), may hold values from -6 to 6
- variance: float32 [8, 8192, 1024], P('replica', 'fsdp'), may hold values from 0.5 to 8
- outer_frag: float32 [8192, 128], P('fsdp'), may hold values from -6 to 6
- outer_mom: float32 [8192, 128], P('fsdp'), may hold values from -6 to 6
- fragment: int32 [1], replicated, may hold values from 0 to 7
Outputs:
- projected: bfloat16 [8, 4096, 1024], P('replica', 'fsdp')
- input_cotangent: bfloat16 [8, 4096, 8192], P('replica', 'fsdp')
- new_weight: float32 [8, 8192, 1024], P('replica', 'fsdp')
- new_moment: float32 [8, 8192, 1024], P('replica', 'fsdp')
- new_variance: float32 [8, 8192, 1024], P('replica', 'fsdp')
- new_outer: float32 [8192, 128], P('fsdp')
- new_momentum: float32 [8192, 128], P('fsdp')
All inputs are finite; a program needn't handle non-finite values.
Results may differ from a plain program's by a relative error of at most 0.0054.
Values may be sent and summed in bfloat16 or wider, within the bound.
A program may use at most 128 MiB of HBM per device.

v0:
```python
import jax
import jax.numpy as jnp
from jax import lax
from jax.sharding import PartitionSpec as P

D = 8192
HD = 128


beta_first = 0.9
beta_second = 0.95
inner_rate = 0.1
decay_rate = 0.1
epsilon = 1e-08
outer_rate = 0.7
outer_beta = 0.9
mixing = 0.5


def contract_rows(left, right):
    return lax.dot_general(
        left, right, (((0,), (0,)), ((), ())), preferred_element_type=jnp.float32
    )


def outer_update(delta, outer_frag, outer_mom):
    groups = lax.axis_size("replica")
    total = lax.psum(delta, "replica")
    average = total / float(groups)
    new_momentum = outer_beta * outer_mom + average
    new_outer = outer_frag - outer_rate * (average + outer_beta * new_momentum)
    return (new_outer, new_momentum)


def shards(activations, cotangent, weight, moment, variance, outer_frag, outer_mom, fragment):
    scale = float(D) ** (-0.5)
    inputs = activations[0]
    upstream = cotangent[0]
    local = weight[0]
    column_start = fragment[0] * HD
    delta = outer_frag - lax.dynamic_slice_in_dim(local, column_start, HD, 1)
    cast = local.astype(jnp.bfloat16)
    piece = lax.all_gather(cast, "fsdp", axis=0, tiled=True)
    features = inputs
    key_total = jnp.dot(features, piece, preferred_element_type=jnp.float32)
    columns = lax.dot_general(
        upstream, piece, (((1,), (1,)), ((), ())), preferred_element_type=jnp.float32
    )
    back_total = columns
    key_total, back_total = (key_total, back_total)
    projected = (key_total * scale).astype(jnp.bfloat16)
    backward = (back_total * scale).astype(jnp.bfloat16)
    features = inputs
    gradient = (
        lax.psum_scatter(
            contract_rows(features, upstream).astype(jnp.bfloat16),
            "fsdp",
            scatter_dimension=0,
            tiled=True,
        ).astype(jnp.float32)
        * scale
    )
    first_new = beta_first * moment[0] + (1.0 - beta_first) * gradient
    second_new = beta_second * variance[0] + (1.0 - beta_second) * gradient * gradient
    stepped = local - inner_rate * (
        first_new / (jnp.sqrt(second_new) + epsilon) + decay_rate * local
    )
    new_outer, new_momentum = outer_update(delta, outer_frag, outer_mom)
    current = lax.dynamic_slice_in_dim(stepped, column_start, HD, 1)
    merged = mixing * current + (1.0 - mixing) * new_outer
    new_weight = lax.dynamic_update_slice_in_dim(stepped, merged, column_start, 1)
    return (
        projected[None],
        backward[None],
        new_weight[None],
        first_new[None],
        second_new[None],
        new_outer,
        new_momentum,
    )


def solution(mesh):
    in_specs = (
        P("replica", "fsdp", None),
        P("replica", "fsdp", None),
        P("replica", "fsdp", None),
        P("replica", "fsdp", None),
        P("replica", "fsdp", None),
        P("fsdp", None),
        P("fsdp", None),
        P(),
    )
    out_specs = (
        P("replica", "fsdp", None),
        P("replica", "fsdp", None),
        P("replica", "fsdp", None),
        P("replica", "fsdp", None),
        P("replica", "fsdp", None),
        P("fsdp", None),
        P("fsdp", None),
    )
    return jax.shard_map(shards, mesh=mesh, in_specs=in_specs, out_specs=out_specs, check_vma=False)
```

profile of v0, /device:TPU:1, one launch (start us, length us, event | category | flops | bytes accessed | tf_op | source)
XLA Modules:
  0.0 328.7 jit_solution(9269899768467339618)
XLA Ops:
  8.0 0.0 copy-start
  8.0 0.0 all-gather.2.cloned.1.call-start
  8.1 2.2 bitcast_convert_fusion
  10.3 0.0 all-gather.2.cloned.1.call-update
  10.3 0.0 reduce-scatter.2.cloned.1.call-start
  10.4 0.0 copy-done
  10.4 9.1 %convolution_convert_fusion = bf16[8192,1024]{1,0:T(8,128)(2,1)} fusion(bf16[1,128,8192]{2,1,0:T(8,128)(2,1)S(1)} %copy-done, bf16[1,128,1024]{2,1,0:T(8,128)(2,1)} %param.9), kind=kOutput, calls=%fused_computation | convolution fusion | flops 2155872256 | bytes 19136512 | tf_op jit(solution)/shard_map/dot_general | solution.py:21
  19.4 0.0 copy-start.1
  19.4 0.0 copy-start.5
  19.5 0.0 reduce-scatter.2.cloned.1.call-update
  19.5 0.0 all-reduce.2.cloned.1.call-start
  20.3 0.4 copy-done.1
  20.7 0.0 copy-done.5
  20.7 0.7 bitcast_subtract_fusion.1
  21.4 0.0 all-reduce.2.cloned.1.call-update
  21.4 0.0 copy-start.3
  21.4 99.1 %all-gather.2.cloned.1.call-done = bf16[8192,1024]{1,0:T(8,128)(2,1)} async-done(((bf16[256,1024]{1,0:T(8,128)(2,1)}), bf16[8192,1024]{1,0:T(8,128)(2,1)}) %all-gather.2.cloned.1.call-update) | async-done | bytes 16777232 | tf_op jit(solution)/shard_map/all_gather | solution.py:43
  120.5 8.8 %fusion.11 = bf16[1,128,1024]{2,1,0:T(8,128)(2,1)} fusion(bf16[8192,1024]{1,0:T(8,128)(2,1)} %all-gather.2.cloned.1.call-done, bf16[1,128,8192]{2,1,0:T(8,128)(2,1)S(1)} %copy-done), kind=kOutput, calls=%fused_computation.12 | convolution fusion | flops 2147745792 | bytes 19136512 | tf_op jit(solution)/shard_map/dot_general | solution.py:45
  129.3 0.0 copy-done.3
  129.3 13.1 %fusion.1 = bf16[1,128,8192]{2,1,0:T(8,128)(2,1)} fusion(bf16[8192,1024]{1,0:T(8,128)(2,1)} %all-gather.2.cloned.1.call-done, bf16[1,128,1024]{2,1,0:T(8,128)(2,1)S(1)} %copy-done.3), kind=kOutput, calls=%fused_computation.3 | convolution fusion | flops 2149580800 | bytes 19136512 | tf_op jit(solution)/shard_map/dot_general | solution.py:46
  142.4 0.0 copy-start.6
  142.4 171.3 %reduce-scatter.2.cloned.1.call-done = bf16[256,1024]{1,0:T(8,128)(2,1)} async-done(((bf16[8192,1024]{1,0:T(8,128)(2,1)}), bf16[256,1024]{1,0:T(8,128)(2,1)}) %reduce-scatter.2.cloned.1.call-update) | async-done | bytes 524304 | tf_op jit(solution)/shard_map/reduce_scatter | solution.py:55
  313.7 3.8 %fusion.20 = (f32[1,256,1024]{2,1,0:T(8,128)}, f32[256,1024]{1,0:T(8,128)S(1)}, f32[1,256,1024]{2,1,0:T(8,128)}) fusion(bf16[256,1024]{1,0:T(8,128)(2,1)} %reduce-scatter.2.cloned.1.call-done, f32[1,256,1024]{2,1,0:T(8,128)} %param.12, f32[1,256,1024]{2,1,0:T(8,128)} %param.11, f32[1,256,1024]{2,1,0:T(8,128)S(1)} %copy-done.1), kind=kLoop, calls=%fused_computation.22 | loop fusion | flops 3932160 | bytes 6815744 | tf_op jit(solution)/shard_map/broadcast_in_dim | solution.py:77
  317.5 0.0 copy-start.2
  317.5 1.0 copy-done.2
  318.5 0.1 copy.16
  318.5 0.0 all-reduce.2.cloned.1.call-done
  318.6 0.0 copy-done.6
  318.6 1.7 bitcast_dynamic-update-slice_fusion
  320.3 0.0 copy-start.4
  320.3 1.0 copy-done.4
Async XLA Ops:
  8.0 2.4 copy-start
  8.0 112.4 %all-gather.2.cloned.1.call-start = ((), (), s32[]{:S(2)}) async-start(), calls=%async_computation.1 | async-start | bytes 17301504 | tf_op jit(solution)/shard_map/all_gather | solution.py:43
  10.3 303.4 %reduce-scatter.2.cloned.1.call-start = ((), (), s32[]{:S(2)}) async-start(), calls=%async_computation.2 | async-start | bytes 17301504 | tf_op jit(solution)/shard_map/reduce_scatter | solution.py:55
  19.4 1.2 copy-start.1
  19.4 1.2 copy-start.5
  19.5 299.1 %all-reduce.2.cloned.1.call-start = ((), (), s32[]{:S(2)}) async-start(), calls=%async_computation.3 | async-start | bytes 262144 | tf_op jit(solution)/shard_map/psum | solution.py:28
  21.4 107.9 %copy-start.3 = (bf16[1,128,1024]{2,1,0:T(8,128)(2,1)S(1)}, bf16[1,128,1024]{2,1,0:T(8,128)(2,1)}, u32[]{:S(2)}) copy-start(bf16[1,128,1024]{2,1,0:T(8,128)(2,1)} %param.9) | copy-start | bytes 786436
  142.4 176.2 %copy-start.6 = (f32[256,128]{1,0:T(8,128)S(1)}, f32[256,128]{1,0:T(8,128)}, u32[]{:S(2)}) copy-start(f32[256,128]{1,0:T(8,128)} %param.14) | copy-start | bytes 393220
  317.5 1.0 copy-start.2
  320.3 1.0 copy-start.4
Sparse Core Ops, SparseCore 0:
  11.3 109.1 all-gather.1
  123.0 190.6 reduce-scatter.1
Sparse Core Ops, SparseCore 1:
  23.1 142.4 all-reduce.1
where the time goes:
time: 332 us; the launch traced here: 329 us
  waiting for transfers between devices  270 us (81%)
  matrix products  31 us (9%)
  between operations  16.3 us (5%)
  other arithmetic  8.42 us (3%)
    reduce_scatter x1, waiting for transfers between devices, shards(): lax.psum_scatter(contract_rows(features, upstream).astype(jnp.bfloat16),...  171 us
    all_gather x1, waiting for transfers between devices, shards(): piece = lax.all_gather(cast, 'fsdp', axis=0, tiled=True)  99.1 us
    dot_general x1, matrix products, shards(): lax.dot_general(upstream, piece, (((1,), (1,)), ((), ())), preferred_elem...  13.1 us
    dot_general x1, matrix products, contract_rows(): lax.dot_general(left, right, (((0,), (0,)), ((), ())), preferred_element_...  9.07 us
    dot_general x1, matrix products, shards(): key_total = jnp.dot(features, piece, preferred_element_type=jnp.float32)  8.82 us
  transfers between devices with their start and end apart: 3, of which 2 were waited for; matrix products, arithmetic and copies ran while one was open for 11% of the time, Pallas kernels for 0%

commit v1 on v0

v1 whole, which is shorter than its diff:
```python
import functools

import jax
import jax.numpy as jnp
from jax import lax
from jax.experimental import pallas as pl
from jax.experimental.pallas import tpu as pltpu
from jax.sharding import PartitionSpec as P

MESH = pl.DeviceIdType.MESH

D = 8192
HD = 128
KW = 1024
TOK = 128
ROWS = 256
SCALE = float(D) ** (-0.5)

beta_first = 0.9
beta_second = 0.95
inner_rate = 0.1
decay_rate = 0.1
epsilon = 1e-08
outer_rate = 0.7
outer_beta = 0.9
mixing = 0.5

F32 = jnp.float32
BF16 = jnp.bfloat16


def step_kernel(
    frag, a_in, c_in, w_in, m_in, v_in, of_in, om_in,
    proj_out, dx_out, nw_out, nm_out, nv_out, no_out, nmom_out,
    acts, cots, wall, wv, mv, vv, ofv, omv, delta, total, gblk, gsend, g_oi, g_ii, g_io,
    part, part_in, psend, p_in, pv, dxs, y_in, zsum, z_in,
    load_sem, own_sem, out_sem, w_send, w_recv, c_send, c_recv, cf_send, cf_recv,
    a_send, a_recv, g_send, oi_recv, ii_recv, io_recv, pc_send, pc_recv, px_send, px_recv,
    dx_send, dx_recv, dx_own, ys_send, ys_recv, zs_send, zs_recv, yg_send, yg_recv,
):
    rep = lax.axis_index("replica")
    fs = lax.axis_index("fsdp")
    y, zh = rep // 2, rep % 2
    x, z, c = fs // 8, (fs // 2) % 4, fs % 2
    t = x * 2 + c
    hi = z // 2
    inner = hi + (z % 2) - 2 * hi * (z % 2)
    p = z + 1 - 2 * (z % 2)
    q = 3 - z
    r = 3 - p

    def at(xx, zz, cc):
        return (rep, xx * 8 + zz * 2 + cc)

    def group(i):
        u = (t + i) % 8
        return u // 2, u % 2

    def other_x(i):
        return (x + i) % 4

    def from_x(i):
        return (x + 4 - i) % 4

    def rep_at(yy, hh):
        return (yy * 2 + hh, fs)

    def remote(src, dst, send, recv, device):
        return pltpu.make_async_remote_copy(
            src_ref=src, dst_ref=dst, send_sem=send, recv_sem=recv, device_id=device, device_id_type=MESH
        )

    def wait_bytes(ref, sem):
        pltpu.make_async_copy(ref, ref, sem).wait()

    order = (q + inner * (r - q), r + inner * (p - r), p + inner * (q - p), z)

    def column(xx, zz, cc):
        return pl.multiple_of(xx * 2048 + zz * 512 + cc * 256, 256)

    def own_rows(index):
        return pl.ds(pl.multiple_of(index * TOK, TOK), TOK)

    load_w = pltpu.make_async_copy(w_in, wv, load_sem.at[0])
    load_of = pltpu.make_async_copy(of_in, ofv, load_sem.at[1])
    load_c = pltpu.make_async_copy(c_in, cots.at[own_rows(t), :], load_sem.at[2])
    load_om = pltpu.make_async_copy(om_in, omv, load_sem.at[3])
    load_m = pltpu.make_async_copy(m_in, mv, load_sem.at[4])
    load_v = pltpu.make_async_copy(v_in, vv, load_sem.at[5])
    for load in (load_w, load_of, load_c, load_om, load_m, load_v):
        load.start()
    own_acts = []
    for b in range(4):
        load = pltpu.make_async_copy(
            a_in.at[:, pl.ds(column(x, b, c), 256)], acts.at[b, own_rows(t), :], own_sem.at[b]
        )
        load.start()
        own_acts.append(load)

    barrier = pltpu.get_barrier_semaphore()

    def greet(device):
        pl.semaphore_signal(barrier, inc=1, device_id=device, device_id_type=MESH)

    for i in range(1, 8):
        gx, gc = group(i)
        greet(at(gx, z, gc))
    greet(at(x, p, c))
    pl.when(inner == 1)(lambda: greet(at(x, q, c)))
    for i in range(1, 4):
        greet(rep_at((y + i) % 4, zh))
    greet(rep_at(y, 1 - zh))

    load_w.wait()
    wall[z] = wv[...].astype(BF16)
    load_of.wait()
    head = frag[0]
    picked = jnp.zeros((ROWS, HD), F32)
    for h in range(8):
        picked = jnp.where(head == h, wv[:, h * HD : (h + 1) * HD], picked)
    delta[...] = ofv[...] - picked

    pl.semaphore_wait(barrier, 12 + inner)

    def send_w(block, device, slot):
        remote(wall.at[block], wall.at[block], w_send.at[slot], w_recv.at[slot], device).start()

    @pl.when(inner == 0)
    def _():
        send_w(z, at(x, p, c), 0)

    @pl.when(inner == 1)
    def _():
        send_w(z, at(x, p, c), 1)
        send_w(z, at(x, q, c), 4)

    for i in (1, 3, 2):
        remote(c_in, cots.at[own_rows(t), :], c_send.at[i], c_recv.at[i], at(other_x(i), z, c)).start()
    remote(c_in, cots.at[own_rows(t), :], cf_send.at[0], cf_recv.at[0], at(x, z, 1 - c)).start()

    for b in order:

        @pl.loop(1, 8)
        def _(i):
            gx, gc = group(i)
            remote(
                a_in.at[:, pl.ds(column(gx, b, gc), 256)], acts.at[b, own_rows(t), :],
                a_send.at[0], a_recv.at[b], at(gx, z, gc),
            ).start()

    def chunk(index):
        return pl.ds(pl.multiple_of(index * 64, 64), 64)

    for i in range(1, 4):
        yy = (y + i) % 4
        remote(delta.at[chunk(yy), :], y_in.at[i], ys_send.at[i], ys_recv.at[i], rep_at(yy, zh)).start()

    for i in (1, 3, 2):
        src = cots.at[own_rows(from_x(i) * 2 + c), :]
        wait_bytes(src, c_recv.at[i])
        remote(src, src, cf_send.at[i], cf_recv.at[i], at(x, z, 1 - c)).start()

    @pl.when(inner == 1)
    def _():
        wait_bytes(wall.at[p], w_recv.at[0])
        send_w(p, at(x, q, c), 5)
        wait_bytes(wall.at[q], w_recv.at[4])
        send_w(q, at(x, p, c), 2)

    @pl.when(inner == 0)
    def _():
        wait_bytes(wall.at[p], w_recv.at[1])

    for i in range(1, 4):
        wait_bytes(y_in.at[i], ys_recv.at[i])
    zsum[...] = ((delta[chunk(y), :] + y_in[1]) + y_in[2]) + y_in[3]
    remote(zsum, z_in, zs_send.at[0], zs_recv.at[0], rep_at(y, 1 - zh)).start()

    load_c.wait()
    for i in range(4):
        wait_bytes(cots.at[own_rows(from_x(i) * 2 + 1 - c), :], cf_recv.at[i])

    def input_cotangent(b):
        @pl.loop(0, 4)
        def _(i):
            rows = pl.ds(pl.multiple_of(i * 256, 256), 256)
            got = lax.dot_general(
                cots[rows, :], wall[b], (((1,), (1,)), ((), ())), preferred_element_type=F32
            )
            dxs[b, rows, :] = (got * SCALE).astype(BF16)

        @pl.loop(1, 8)
        def _(i):
            gx, gc = group(i)
            remote(
                dxs.at[b, own_rows(gx * 2 + gc), :], dx_out.at[:, pl.ds(column(x, b, c), 256)],
                dx_send.at[0], dx_recv.at[0], at(gx, z, gc),
            ).start()

        pltpu.make_async_copy(
            dxs.at[b, own_rows(t), :], dx_out.at[:, pl.ds(column(x, b, c), 256)], dx_own.at[b]
        ).start()

    def gradient(k):
        b = order[k]
        pltpu.make_async_copy(
            a_in.at[:, pl.ds(column(x, b, c), 256)], acts.at[b, own_rows(t), :], own_sem.at[b]
        ).wait()
        wait_bytes(acts.at[b, pl.ds(0, 7 * TOK), :], a_recv.at[b])

        @pl.loop(0, 4)
        def _(i):
            cols = pl.ds(pl.multiple_of(i * 256, 256), 256)
            gblk[k, :, cols] = lax.dot_general(
                acts[b], cots[:, cols], (((0,), (0,)), ((), ())), preferred_element_type=F32
            )

    def send_g(k, land, recv, device):
        remote(gsend.at[k], land, g_send.at[k], recv, device).start()

    def outer_send(k):
        @pl.when(inner == 0)
        def _():
            gsend[k] = gblk[k].astype(BF16)
            send_g(k, g_oi.at[k], oi_recv.at[k], at(x, p, c))

    input_cotangent(z)
    gradient(0)
    outer_send(0)
    input_cotangent(p)
    gradient(1)
    outer_send(1)

    @pl.when(inner == 1)
    def _():
        wait_bytes(wall.at[r], w_recv.at[5])
        send_w(r, at(x, p, c), 3)

    @pl.when(inner == 0)
    def _():
        wait_bytes(wall.at[r], w_recv.at[2])

    wait_bytes(z_in, zs_recv.at[0])
    total[chunk(y), :] = zsum[...] + z_in[...]
    for i in range(1, 4):
        remote(
            total.at[chunk(y), :], total.at[chunk(y), :], yg_send.at[i], yg_recv.at[i],
            rep_at((y + i) % 4, zh),
        ).start()

    gradient(2)
    outer_send(2)

    @pl.when(inner == 1)
    def _():
        wait_bytes(g_oi.at[0], oi_recv.at[0])
        gsend[0] = (gblk[0] + g_oi[0].astype(F32)).astype(BF16)
        send_g(0, g_ii.at[0], ii_recv.at[0], at(x, q, c))

    input_cotangent(r + inner * (q - r))
    gradient(3)

    @pl.when(inner == 0)
    def _():
        wait_bytes(wall.at[q], w_recv.at[3])

    @pl.loop(0, 4)
    def _(i):
        rows = pl.ds(pl.multiple_of(i * 256, 256), 256)
        got = jnp.dot(acts[0, rows, :], wall[0], preferred_element_type=F32)
        for b in range(1, 4):
            got += jnp.dot(acts[b, rows, :], wall[b], preferred_element_type=F32)
        part[i] = got
        remote(
            part.at[i, own_rows(1 - c), :], part_in.at[i], pc_send.at[i], pc_recv.at[i], at(x, z, 1 - c)
        ).start()

    @pl.when(inner == 1)
    def _():
        wait_bytes(g_ii.at[0], ii_recv.at[0])
        gsend[1] = (gblk[1] + g_ii[0].astype(F32)).astype(BF16)
        send_g(1, g_io, io_recv.at[0], at(x, p, c))

    for i in (1, 3, 2):
        xx = other_x(i)
        wait_bytes(part_in.at[xx], pc_recv.at[xx])
        psend[i] = (part[xx, own_rows(c), :] + part_in[xx]).astype(BF16)
        remote(psend.at[i], p_in.at[i], px_send.at[i], px_recv.at[i], at(xx, z, c)).start()
    input_cotangent(q + inner * (r - q))

    @pl.when(inner == 1)
    def _():
        wait_bytes(g_oi.at[1], oi_recv.at[1])
        gsend[2] = (gblk[2] + g_oi[1].astype(F32)).astype(BF16)
        send_g(2, g_ii.at[1], ii_recv.at[1], at(x, q, c))

    for i in range(1, 4):
        wait_bytes(total.at[chunk((y + 4 - i) % 4), :], yg_recv.at[i])
    load_om.wait()
    average = total[...] / 8.0
    momentum = outer_beta * omv[...] + average
    fresh = ofv[...] - outer_rate * (average + outer_beta * momentum)
    omv[...] = momentum
    ofv[...] = fresh
    outs = [
        pltpu.make_async_copy(ofv, no_out, out_sem.at[0]),
        pltpu.make_async_copy(omv, nmom_out, out_sem.at[1]),
    ]
    for out in outs:
        out.start()

    @pl.when(inner == 0)
    def _():
        wait_bytes(g_io, io_recv.at[0])
        gblk[3] = gblk[3] + g_io[...].astype(F32)

    @pl.when(inner == 1)
    def _():
        wait_bytes(g_oi.at[2], oi_recv.at[2])
        wait_bytes(g_ii.at[1], ii_recv.at[1])
        gblk[3] = gblk[3] + g_oi[2].astype(F32) + g_ii[1].astype(F32)

    load_m.wait()
    load_v.wait()

    @pl.loop(0, 8)
    def _(i):
        rows = pl.ds(pl.multiple_of(i * 32, 32), 32)
        for h in range(8):
            cols = slice(h * HD, (h + 1) * HD)
            grad = gblk[3, rows, cols] * SCALE
            first = beta_first * mv[rows, cols] + (1.0 - beta_first) * grad
            second = beta_second * vv[rows, cols] + (1.0 - beta_second) * grad * grad
            local = wv[rows, cols]
            stepped = local - inner_rate * (first / (jnp.sqrt(second) + epsilon) + decay_rate * local)
            merged = mixing * stepped + (1.0 - mixing) * ofv[rows, :]
            mv[rows, cols] = first
            vv[rows, cols] = second
            wv[rows, cols] = jnp.where(head == h, merged, stepped)

    more = [
        pltpu.make_async_copy(wv, nw_out, out_sem.at[2]),
        pltpu.make_async_copy(mv, nm_out, out_sem.at[3]),
        pltpu.make_async_copy(vv, nv_out, out_sem.at[4]),
    ]
    for out in more:
        out.start()

    wait_bytes(part_in.at[x], pc_recv.at[x])
    for i in (1, 3, 2):
        wait_bytes(p_in.at[i], px_recv.at[i])
    got = part[x, own_rows(c), :] + part_in[x]
    for i in (1, 3, 2):
        got += p_in[i].astype(F32)
    pv[...] = (got * SCALE).astype(BF16)
    last = pltpu.make_async_copy(pv, proj_out, out_sem.at[5])
    last.start()

    @pl.when(inner == 0)
    def _():
        wait_bytes(wall.at[z], w_send.at[0])

    @pl.when(inner == 1)
    def _():
        for slot in range(1, 6):
            wait_bytes(wall.at[z], w_send.at[slot])

    for i in range(1, 4):
        wait_bytes(cots.at[own_rows(t), :], c_send.at[i])
        wait_bytes(psend.at[i], px_send.at[i])
        wait_bytes(delta.at[chunk(0), :], ys_send.at[i])
        wait_bytes(total.at[chunk(0), :], yg_send.at[i])
    wait_bytes(zsum, zs_send.at[0])
    for i in range(4):
        wait_bytes(cots.at[own_rows(t), :], cf_send.at[i])
        wait_bytes(part_in.at[i], pc_send.at[i])
    for k in range(3):
        wait_bytes(gsend.at[k], g_send.at[k])
    wait_bytes(dx_out.at[:, pl.ds(0, 28 * 256)], a_send.at[0])
    for out in (*outs, *more, last):
        out.wait()
    for b in range(4):
        wait_bytes(dxs.at[b, own_rows(t), :], dx_own.at[b])
    wait_bytes(dx_out.at[:, pl.ds(0, 28 * 256)], dx_send.at[0])
    wait_bytes(dx_out.at[:, pl.ds(0, 28 * 256)], dx_recv.at[0])


def finish_kernel(*refs):
    n = (len(refs) - 1) // 2
    sem = refs[-1]
    copies = [pltpu.make_async_copy(refs[i], refs[n + i], sem.at[i]) for i in range(n)]
    for copy in copies:
        copy.start()
    for copy in copies:
        copy.wait()


ANY = pl.BlockSpec(memory_space=pl.ANY)


def shards(activations, cotangent, weight, moment, variance, outer_frag, outer_mom, fragment):
    results = (
        ((TOK, KW), BF16),
        ((TOK, D), BF16),
        ((ROWS, KW), F32),
        ((ROWS, KW), F32),
        ((ROWS, KW), F32),
        ((ROWS, HD), F32),
        ((ROWS, HD), F32),
    )
    dma = pltpu.SemaphoreType.DMA
    outs = pl.pallas_call(
        step_kernel,
        out_shape=[pltpu.VMEM(shape, dtype) for shape, dtype in results],
        in_specs=[pl.BlockSpec(memory_space=pltpu.SMEM)] + [ANY] * 7,
        out_specs=[ANY] * 7,
        scratch_shapes=[
            pltpu.VMEM((4, 1024, 256), BF16),
            pltpu.VMEM((1024, KW), BF16),
            pltpu.VMEM((4, ROWS, KW), BF16),
            pltpu.VMEM((ROWS, KW), F32),
            pltpu.VMEM((ROWS, KW), F32),
            pltpu.VMEM((ROWS, KW), F32),
            pltpu.VMEM((ROWS, HD), F32),
            pltpu.VMEM((ROWS, HD), F32),
            pltpu.VMEM((ROWS, HD), F32),
            pltpu.VMEM((ROWS, HD), F32),
            pltpu.VMEM((4, ROWS, KW), F32),
            pltpu.VMEM((3, ROWS, KW), BF16),
            pltpu.VMEM((3, ROWS, KW), BF16),
            pltpu.VMEM((2, ROWS, KW), BF16),
            pltpu.VMEM((ROWS, KW), BF16),
            pltpu.VMEM((4, 256, KW), F32),
            pltpu.VMEM((4, TOK, KW), F32),
            pltpu.VMEM((4, TOK, KW), BF16),
            pltpu.VMEM((4, TOK, KW), BF16),
            pltpu.VMEM((TOK, KW), BF16),
            pltpu.VMEM((4, 1024, 256), BF16),
            pltpu.VMEM((4, 64, HD), F32),
            pltpu.VMEM((64, HD), F32),
            pltpu.VMEM((64, HD), F32),
            dma((6,)),
            dma((4,)),
            dma((6,)),
            dma((6,)),
            dma((6,)),
            dma((4,)),
            dma((4,)),
            dma((4,)),
            dma((4,)),
            dma((1,)),
            dma((4,)),
            dma((3,)),
            dma((3,)),
            dma((2,)),
            dma((1,)),
            dma((4,)),
            dma((4,)),
            dma((4,)),
            dma((4,)),
            dma((1,)),
            dma((1,)),
            dma((4,)),
            dma((4,)),
            dma((4,)),
            dma((1,)),
            dma((1,)),
            dma((4,)),
            dma((4,)),
        ],
        compiler_params=pltpu.CompilerParams(
            collective_id=0, has_side_effects=True, vmem_limit_bytes=40 * 2**20
        ),
    )(
        fragment,
        *(
            pltpu.with_memory_space_constraint(a, pltpu.HBM)
            for a in (
                activations[0], cotangent[0], weight[0], moment[0], variance[0], outer_frag, outer_mom
            )
        ),
    )
    outs = pl.pallas_call(
        finish_kernel,
        out_shape=[pltpu.HBM(shape, dtype) for shape, dtype in results],
        in_specs=[ANY] * 7,
        out_specs=[ANY] * 7,
        scratch_shapes=[dma((7,))],
        compiler_params=pltpu.CompilerParams(vmem_limit_bytes=2 * 2**20),
    )(*(pltpu.with_memory_space_constraint(a, pltpu.VMEM) for a in outs))
    return tuple(out[None] for out in outs[:5]) + tuple(outs[5:])


def solution(mesh):
    split = P("replica", "fsdp", None)
    return jax.shard_map(
        shards,
        mesh=mesh,
        in_specs=(split, split, split, split, split, P("fsdp", None), P("fsdp", None), P()),
        out_specs=(split, split, split, split, split, P("fsdp", None), P("fsdp", None)),
        check_vma=False,
    )
```

time: 332 us -> 84.3 us (0.25)
  waiting for transfers between devices: 270 us -> 0 us
  Pallas kernels: 0 us -> 83 us
  matrix products: 31 us -> 0 us
  between operations: 16.3 us -> 1.29 us
  other arithmetic: 8.42 us -> 0 us
    reduce_scatter x1 -> x0, waiting for transfers between devices: 171 us -> none  [shards(): lax.psum_scatter(contract_rows(features, upstream).astype(jnp.bfloat16),...]
    all_gather x1 -> x0, waiting for transfers between devices: 99.1 us -> none  [shards(): piece = lax.all_gather(cast, 'fsdp', axis=0, tiled=True)]
    pallas_call x0 -> x2, Pallas kernels: none -> 83 us  [the longest x1 80.4 us: shards(): pl.pallas_call(step_kernel, out_shape=[pltpu.VMEM(shape, dtype) for shape...]
    dot_general x3 -> x0, matrix products: 31 us -> none  [the longest x1 13.1 us: shards(): lax.dot_general(upstream, piece, (((1,), (1,)), ((), ())), preferred_elem...]
    broadcast_in_dim x1 -> x0, other arithmetic: 3.79 us -> none  [shards(): second_new[None]]
  transfers between devices with their start and end apart: 3 -> 0, of which waited for: 2 -> 0; matrix products, arithmetic and copies ran while one was open for 11% -> 0% of each run, Pallas kernels for 0% -> 0%
where the time goes in v1:
time: 84.3 us; the launch traced here: 84.2 us
  Pallas kernels  83 us (98%)
  between operations  1.29 us (2%)
    pallas_call x1, Pallas kernels, shards(): pl.pallas_call(step_kernel, out_shape=[pltpu.VMEM(shape, dtype) for shape...  80.4 us
    pallas_call x1, Pallas kernels, shards(): pl.pallas_call(finish_kernel, out_shape=[pltpu.HBM(shape, dtype) for shap...  2.54 us

profile of v1, /device:TPU:1, one launch (start us, length us, event | category | flops | bytes accessed | tf_op | source)
XLA Modules:
  0.0 84.2 jit_solution(7175234609446947145)
XLA Ops:
  1.3 80.4 %shard_map.135 = (bf16[128,1024]{1,0:T(8,128)(2,1)S(1)}, bf16[128,8192]{1,0:T(8,128)(2,1)S(1)}, f32[256,1024]{1,0:T(8,128)S(1)}, f32[256,1024]{1,0:T(8,128)S(1)}...) custom-call(s32[1]{0:T(128)S(6)} %copy.15.frag, bf16[128,8192]{1,0:T(8,128)(2,1)} %bitcast.10, ...), custom_call_target="tpu_custom_call" | custom-call | tf_op jit(solution)/shard_map/pallas_call | solution.py:412
  81.7 2.5 %shard_map.136 = (bf16[128,1024]{1,0:T(8,128)(2,1)}, bf16[128,8192]{1,0:T(8,128)(2,1)}, f32[256,1024]{1,0:T(8,128)}, f32[256,1024]{1,0:T(8,128)}, f32[256,1024]{...) custom-call(bf16[128,1024]{1,0:T(8,128)(2,1)S(1)} %get-tuple-element.21.refs_0_, ...), custom_call_target="tpu_custom_call" | custom-call | tf_op jit(solution)/shard_map/pallas_call | solution.py:483

commit v2 on v1

--- a/solution.py
+++ b/solution.py
@@ -33,8 +33,8 @@
     frag, a_in, c_in, w_in, m_in, v_in, of_in, om_in,
     proj_out, dx_out, nw_out, nm_out, nv_out, no_out, nmom_out,
     acts, cots, wall, wv, mv, vv, ofv, omv, delta, total, gblk, gsend, g_oi, g_ii, g_io,
-    part, part_in, psend, p_in, pv, dxs, y_in, zsum, z_in,
-    load_sem, own_sem, out_sem, w_send, w_recv, c_send, c_recv, cf_send, cf_recv,
+    part, part_in, psend, p_in, dxs, y_in, zsum, z_in,
+    load_sem, own_sem, w_send, w_recv, c_send, c_recv, cf_send, cf_recv,
     a_send, a_recv, g_send, oi_recv, ii_recv, io_recv, pc_send, pc_recv, px_send, px_recv,
     dx_send, dx_recv, dx_own, ys_send, ys_recv, zs_send, zs_recv, yg_send, yg_recv,
 ):
@@ -59,9 +59,6 @@
     def other_x(i):
         return (x + i) % 4
 
-    def from_x(i):
-        return (x + 4 - i) % 4
-
     def rep_at(yy, hh):
         return (yy * 2 + hh, fs)
 
@@ -74,6 +71,9 @@
         pltpu.make_async_copy(ref, ref, sem).wait()
 
     order = (q + inner * (r - q), r + inner * (p - r), p + inner * (q - p), z)
+
+    def block(b):
+        return pl.ds(pl.multiple_of(b * 256, 256), 256)
 
     def column(xx, zz, cc):
         return pl.multiple_of(xx * 2048 + zz * 512 + cc * 256, 256)
@@ -92,7 +92,7 @@
     own_acts = []
     for b in range(4):
         load = pltpu.make_async_copy(
-            a_in.at[:, pl.ds(column(x, b, c), 256)], acts.at[b, own_rows(t), :], own_sem.at[b]
+            a_in.at[:, pl.ds(column(x, b, c), 256)], acts.at[own_rows(t), block(b)], own_sem.at[b]
         )
         load.start()
         own_acts.append(load)
@@ -109,10 +109,9 @@
     pl.when(inner == 1)(lambda: greet(at(x, q, c)))
     for i in range(1, 4):
         greet(rep_at((y + i) % 4, zh))
-    greet(rep_at(y, 1 - zh))
 
     load_w.wait()
-    wall[z] = wv[...].astype(BF16)
+    wall[block(z), :] = wv[...].astype(BF16)
     load_of.wait()
     head = frag[0]
     picked = jnp.zeros((ROWS, HD), F32)
@@ -120,10 +119,11 @@
         picked = jnp.where(head == h, wv[:, h * HD : (h + 1) * HD], picked)
     delta[...] = ofv[...] - picked
 
-    pl.semaphore_wait(barrier, 12 + inner)
-
-    def send_w(block, device, slot):
-        remote(wall.at[block], wall.at[block], w_send.at[slot], w_recv.at[slot], device).start()
+    pl.semaphore_wait(barrier, 11 + inner + zh)
+    greet(rep_at(y, 1 - zh))
+
+    def send_w(b, device, slot):
+        remote(wall.at[block(b), :], wall.at[block(b), :], w_send.at[slot], w_recv.at[slot], device).start()
 
     @pl.when(inner == 0)
     def _():
@@ -134,19 +134,26 @@
         send_w(z, at(x, p, c), 1)
         send_w(z, at(x, q, c), 4)
 
-    for i in (1, 3, 2):
-        remote(c_in, cots.at[own_rows(t), :], c_send.at[i], c_recv.at[i], at(other_x(i), z, c)).start()
+    right, left = other_x(1), other_x(3)
+    far = other_x(2)
+
+    def half(index, side):
+        return pl.ds(pl.multiple_of(index * TOK + side * 64, 64), 64)
+
+    for slot, device in ((0, at(right, z, c)), (1, at(left, z, c))):
+        remote(c_in, cots.at[own_rows(t), :], c_send.at[slot], c_recv.at[slot], device).start()
     remote(c_in, cots.at[own_rows(t), :], cf_send.at[0], cf_recv.at[0], at(x, z, 1 - c)).start()
 
-    for b in order:
-
+    def send_acts(b):
         @pl.loop(1, 8)
         def _(i):
             gx, gc = group(i)
             remote(
-                a_in.at[:, pl.ds(column(gx, b, gc), 256)], acts.at[b, own_rows(t), :],
+                a_in.at[:, pl.ds(column(gx, b, gc), 256)], acts.at[own_rows(t), block(b)],
                 a_send.at[0], a_recv.at[b], at(gx, z, gc),
             ).start()
+
+    send_acts(order[0])
 
     def chunk(index):
         return pl.ds(pl.multiple_of(index * 64, 64), 64)
@@ -155,40 +162,63 @@
         yy = (y + i) % 4
         remote(delta.at[chunk(yy), :], y_in.at[i], ys_send.at[i], ys_recv.at[i], rep_at(yy, zh)).start()
 
-    for i in (1, 3, 2):
-        src = cots.at[own_rows(from_x(i) * 2 + c), :]
-        wait_bytes(src, c_recv.at[i])
-        remote(src, src, cf_send.at[i], cf_recv.at[i], at(x, z, 1 - c)).start()
-
-    @pl.when(inner == 1)
-    def _():
-        wait_bytes(wall.at[p], w_recv.at[0])
+    for slot, source, device in ((0, left, at(right, z, c)), (1, right, at(left, z, c))):
+        rows = own_rows(source * 2 + c)
+        part_rows = half(source * 2 + c, slot)
+        wait_bytes(cots.at[rows, :], c_recv.at[slot])
+        remote(
+            cots.at[part_rows, :], cots.at[part_rows, :], c_send.at[2 + slot], c_recv.at[2 + slot], device
+        ).start()
+        remote(
+            cots.at[rows, :], cots.at[rows, :], cf_send.at[1 + slot], cf_recv.at[1 + slot], at(x, z, 1 - c)
+        ).start()
+    send_acts(order[1])
+
+    @pl.when(inner == 1)
+    def _():
+        wait_bytes(wall.at[block(p), :], w_recv.at[0])
         send_w(p, at(x, q, c), 5)
-        wait_bytes(wall.at[q], w_recv.at[4])
+        wait_bytes(wall.at[block(q), :], w_recv.at[4])
         send_w(q, at(x, p, c), 2)
 
     @pl.when(inner == 0)
     def _():
-        wait_bytes(wall.at[p], w_recv.at[1])
+        wait_bytes(wall.at[block(p), :], w_recv.at[1])
+
+    def wait_acts(k):
+        b = order[k]
+        pltpu.make_async_copy(
+            a_in.at[:, pl.ds(column(x, b, c), 256)], acts.at[own_rows(t), block(b)], own_sem.at[b]
+        ).wait()
+        wait_bytes(acts.at[pl.ds(0, 7 * TOK), block(b)], a_recv.at[b])
+
+    wait_acts(0)
+    send_acts(order[2])
 
     for i in range(1, 4):
         wait_bytes(y_in.at[i], ys_recv.at[i])
     zsum[...] = ((delta[chunk(y), :] + y_in[1]) + y_in[2]) + y_in[3]
+    @pl.when(zh == 0)
+    def _():
+        pl.semaphore_wait(barrier, 1)
+
     remote(zsum, z_in, zs_send.at[0], zs_recv.at[0], rep_at(y, 1 - zh)).start()
 
+    for slot in (0, 1):
+        wait_bytes(cots.at[half(far * 2 + c, slot), :], c_recv.at[2 + slot])
+    rows = own_rows(far * 2 + c)
+    remote(cots.at[rows, :], cots.at[rows, :], cf_send.at[3], cf_recv.at[3], at(x, z, 1 - c)).start()
     load_c.wait()
-    for i in range(4):
-        wait_bytes(cots.at[own_rows(from_x(i) * 2 + 1 - c), :], cf_recv.at[i])
+    for slot, source in enumerate((x, left, right, far)):
+        wait_bytes(cots.at[own_rows(source * 2 + 1 - c), :], cf_recv.at[slot])
 
     def input_cotangent(b):
-        @pl.loop(0, 4)
-        def _(i):
-            rows = pl.ds(pl.multiple_of(i * 256, 256), 256)
-            got = lax.dot_general(
-                cots[rows, :], wall[b], (((1,), (1,)), ((), ())), preferred_element_type=F32
-            )
-            dxs[b, rows, :] = (got * SCALE).astype(BF16)
-
+        got = lax.dot_general(
+            cots[...], wall[block(b), :], (((1,), (1,)), ((), ())), preferred_element_type=F32
+        )
+        dxs[b] = (got * SCALE).astype(BF16)
+
+    def send_cotangent(b):
         @pl.loop(1, 8)
         def _(i):
             gx, gc = group(i)
@@ -203,17 +233,10 @@
 
     def gradient(k):
         b = order[k]
-        pltpu.make_async_copy(
-            a_in.at[:, pl.ds(column(x, b, c), 256)], acts.at[b, own_rows(t), :], own_sem.at[b]
-        ).wait()
-        wait_bytes(acts.at[b, pl.ds(0, 7 * TOK), :], a_recv.at[b])
-
-        @pl.loop(0, 4)
-        def _(i):
-            cols = pl.ds(pl.multiple_of(i * 256, 256), 256)
-            gblk[k, :, cols] = lax.dot_general(
-                acts[b], cots[:, cols], (((0,), (0,)), ((), ())), preferred_element_type=F32
-            )
+
+        gblk[k] = lax.dot_general(
+            acts[:, block(b)], cots[...], (((0,), (0,)), ((), ())), preferred_element_type=F32
+        )
 
     def send_g(k, land, recv, device):
         remote(gsend.at[k], land, g_send.at[k], recv, device).start()
@@ -224,21 +247,23 @@
             gsend[k] = gblk[k].astype(BF16)
             send_g(k, g_oi.at[k], oi_recv.at[k], at(x, p, c))
 
-    input_cotangent(z)
     gradient(0)
     outer_send(0)
-    input_cotangent(p)
+    wait_acts(1)
+    send_acts(order[3])
     gradient(1)
     outer_send(1)
 
     @pl.when(inner == 1)
     def _():
-        wait_bytes(wall.at[r], w_recv.at[5])
+        wait_bytes(wall.at[block(r), :], w_recv.at[5])
         send_w(r, at(x, p, c), 3)
 
     @pl.when(inner == 0)
     def _():
-        wait_bytes(wall.at[r], w_recv.at[2])
+        wait_bytes(wall.at[block(r), :], w_recv.at[2])
+
+    input_cotangent(z)
 
     wait_bytes(z_in, zs_recv.at[0])
     total[chunk(y), :] = zsum[...] + z_in[...]
@@ -248,8 +273,14 @@
             rep_at((y + i) % 4, zh),
         ).start()
 
+    wait_acts(2)
+    send_cotangent(z)
     gradient(2)
     outer_send(2)
+    third = r + inner * (q - r)
+    fourth = q + inner * (r - q)
+    input_cotangent(p)
+    input_cotangent(third)
 
     @pl.when(inner == 1)
     def _():
@@ -257,42 +288,65 @@
         gsend[0] = (gblk[0] + g_oi[0].astype(F32)).astype(BF16)
         send_g(0, g_ii.at[0], ii_recv.at[0], at(x, q, c))
 
-    input_cotangent(r + inner * (q - r))
-    gradient(3)
-
-    @pl.when(inner == 0)
-    def _():
-        wait_bytes(wall.at[q], w_recv.at[3])
+    wait_acts(3)
+    send_cotangent(p)
 
     @pl.loop(0, 4)
     def _(i):
-        rows = pl.ds(pl.multiple_of(i * 256, 256), 256)
-        got = jnp.dot(acts[0, rows, :], wall[0], preferred_element_type=F32)
-        for b in range(1, 4):
-            got += jnp.dot(acts[b, rows, :], wall[b], preferred_element_type=F32)
+        got = jnp.dot(acts[block(i), block(z)], wall[block(z), :], preferred_element_type=F32)
+        for b in (p, third):
+            got += jnp.dot(acts[block(i), block(b)], wall[block(b), :], preferred_element_type=F32)
         part[i] = got
+
+    @pl.when(inner == 0)
+    def _():
+        wait_bytes(wall.at[block(q), :], w_recv.at[3])
+
+    def partial(xx):
+        part[xx] += jnp.dot(
+            acts[block(xx), block(fourth)], wall[block(fourth), :], preferred_element_type=F32
+        )
         remote(
-            part.at[i, own_rows(1 - c), :], part_in.at[i], pc_send.at[i], pc_recv.at[i], at(x, z, 1 - c)
+            part.at[xx, own_rows(1 - c), :], part_in.at[xx], pc_send.at[xx], pc_recv.at[xx], at(x, z, 1 - c)
         ).start()
+
+    @pl.loop(0, 2)
+    def _(i):
+        partial((x + 2 - i) % 4)
+
+    wait_bytes(part_in.at[far], pc_recv.at[far])
+    psend[2] = (part[far, own_rows(c), :] + part_in[far]).astype(BF16)
+    for slot, device in ((0, at(right, z, c)), (1, at(left, z, c))):
+        rows = pl.ds(slot * 64, 64)
+        remote(psend.at[2, rows, :], p_in.at[2, rows, :], px_send.at[2 + slot], px_recv.at[2 + slot], device).start()
+
+    @pl.loop(0, 2)
+    def _(i):
+        partial((x + 3 + i) % 4)
+
+    send_cotangent(third)
+    gradient(3)
+    input_cotangent(fourth)
 
     @pl.when(inner == 1)
     def _():
         wait_bytes(g_ii.at[0], ii_recv.at[0])
         gsend[1] = (gblk[1] + g_ii[0].astype(F32)).astype(BF16)
         send_g(1, g_io, io_recv.at[0], at(x, p, c))
-
-    for i in (1, 3, 2):
-        xx = other_x(i)
-        wait_bytes(part_in.at[xx], pc_recv.at[xx])
-        psend[i] = (part[xx, own_rows(c), :] + part_in[xx]).astype(BF16)
-        remote(psend.at[i], p_in.at[i], px_send.at[i], px_recv.at[i], at(xx, z, c)).start()
-    input_cotangent(q + inner * (r - q))
-
-    @pl.when(inner == 1)
-    def _():
         wait_bytes(g_oi.at[1], oi_recv.at[1])
         gsend[2] = (gblk[2] + g_oi[1].astype(F32)).astype(BF16)
         send_g(2, g_ii.at[1], ii_recv.at[1], at(x, q, c))
+
+    for slot, target in ((0, right), (1, left)):
+        rows = pl.ds(slot * 64, 64)
+        wait_bytes(part_in.at[target], pc_recv.at[target])
+        wait_bytes(p_in.at[2, rows, :], px_recv.at[2 + slot])
+        both = part[target, own_rows(c), :] + part_in[target]
+        psend[slot] = both.astype(BF16)
+        psend[slot, rows, :] = (both[slot * 64 : slot * 64 + 64] + p_in[2, rows, :].astype(F32)).astype(BF16)
+        remote(psend.at[slot], p_in.at[slot], px_send.at[slot], px_recv.at[slot], at(target, z, c)).start()
+
+    send_cotangent(fourth)
 
     for i in range(1, 4):
         wait_bytes(total.at[chunk((y + 4 - i) % 4), :], yg_recv.at[i])
@@ -300,14 +354,8 @@
     average = total[...] / 8.0
     momentum = outer_beta * omv[...] + average
     fresh = ofv[...] - outer_rate * (average + outer_beta * momentum)
-    omv[...] = momentum
-    ofv[...] = fresh
-    outs = [
-        pltpu.make_async_copy(ofv, no_out, out_sem.at[0]),
-        pltpu.make_async_copy(omv, nmom_out, out_sem.at[1]),
-    ]
-    for out in outs:
-        out.start()
+    nmom_out[...] = momentum
+    no_out[...] = fresh
 
     @pl.when(inner == 0)
     def _():
@@ -333,52 +381,42 @@
             second = beta_second * vv[rows, cols] + (1.0 - beta_second) * grad * grad
             local = wv[rows, cols]
             stepped = local - inner_rate * (first / (jnp.sqrt(second) + epsilon) + decay_rate * local)
-            merged = mixing * stepped + (1.0 - mixing) * ofv[rows, :]
-            mv[rows, cols] = first
-            vv[rows, cols] = second
-            wv[rows, cols] = jnp.where(head == h, merged, stepped)
-
-    more = [
-        pltpu.make_async_copy(wv, nw_out, out_sem.at[2]),
-        pltpu.make_async_copy(mv, nm_out, out_sem.at[3]),
-        pltpu.make_async_copy(vv, nv_out, out_sem.at[4]),
-    ]
-    for out in more:
-        out.start()
+            merged = mixing * stepped + (1.0 - mixing) * no_out[rows, :]
+            nm_out[rows, cols] = first
+            nv_out[rows, cols] = second
+            nw_out[rows, cols] = jnp.where(head == h, merged, stepped)
 
     wait_bytes(part_in.at[x], pc_recv.at[x])
-    for i in (1, 3, 2):
-        wait_bytes(p_in.at[i], px_recv.at[i])
     got = part[x, own_rows(c), :] + part_in[x]
-    for i in (1, 3, 2):
-        got += p_in[i].astype(F32)
-    pv[...] = (got * SCALE).astype(BF16)
-    last = pltpu.make_async_copy(pv, proj_out, out_sem.at[5])
-    last.start()
+    for slot in (0, 1):
+        wait_bytes(p_in.at[slot], px_recv.at[slot])
+        got += p_in[slot].astype(F32)
+    proj_out[...] = (got * SCALE).astype(BF16)
 
     @pl.when(inner == 0)
     def _():
-        wait_bytes(wall.at[z], w_send.at[0])
+        wait_bytes(wall.at[block(z), :], w_send.at[0])
 
     @pl.when(inner == 1)
     def _():
         for slot in range(1, 6):
-            wait_bytes(wall.at[z], w_send.at[slot])
+            wait_bytes(wall.at[block(z), :], w_send.at[slot])
 
     for i in range(1, 4):
-        wait_bytes(cots.at[own_rows(t), :], c_send.at[i])
-        wait_bytes(psend.at[i], px_send.at[i])
         wait_bytes(delta.at[chunk(0), :], ys_send.at[i])
         wait_bytes(total.at[chunk(0), :], yg_send.at[i])
     wait_bytes(zsum, zs_send.at[0])
+    for slot in (0, 1):
+        wait_bytes(cots.at[own_rows(t), :], c_send.at[slot])
+        wait_bytes(cots.at[half(t, 0), :], c_send.at[2 + slot])
+        wait_bytes(psend.at[slot], px_send.at[slot])
+        wait_bytes(psend.at[2, pl.ds(0, 64), :], px_send.at[2 + slot])
     for i in range(4):
         wait_bytes(cots.at[own_rows(t), :], cf_send.at[i])
         wait_bytes(part_in.at[i], pc_send.at[i])
     for k in range(3):
         wait_bytes(gsend.at[k], g_send.at[k])
     wait_bytes(dx_out.at[:, pl.ds(0, 28 * 256)], a_send.at[0])
-    for out in (*outs, *more, last):
-        out.wait()
     for b in range(4):
         wait_bytes(dxs.at[b, own_rows(t), :], dx_own.at[b])
     wait_bytes(dx_out.at[:, pl.ds(0, 28 * 256)], dx_send.at[0])
@@ -413,11 +451,11 @@
         step_kernel,
         out_shape=[pltpu.VMEM(shape, dtype) for shape, dtype in results],
         in_specs=[pl.BlockSpec(memory_space=pltpu.SMEM)] + [ANY] * 7,
-        out_specs=[ANY] * 7,
+        out_specs=[pl.BlockSpec(memory_space=pltpu.VMEM)] * 7,
         scratch_shapes=[
-            pltpu.VMEM((4, 1024, 256), BF16),
+            pltpu.VMEM((1024, 1024), BF16),
             pltpu.VMEM((1024, KW), BF16),
-            pltpu.VMEM((4, ROWS, KW), BF16),
+            pltpu.VMEM((1024, KW), BF16),
             pltpu.VMEM((ROWS, KW), F32),
             pltpu.VMEM((ROWS, KW), F32),
             pltpu.VMEM((ROWS, KW), F32),
@@ -432,16 +470,14 @@
             pltpu.VMEM((ROWS, KW), BF16),
             pltpu.VMEM((4, 256, KW), F32),
             pltpu.VMEM((4, TOK, KW), F32),
-            pltpu.VMEM((4, TOK, KW), BF16),
-            pltpu.VMEM((4, TOK, KW), BF16),
-            pltpu.VMEM((TOK, KW), BF16),
+            pltpu.VMEM((3, TOK, KW), BF16),
+            pltpu.VMEM((3, TOK, KW), BF16),
             pltpu.VMEM((4, 1024, 256), BF16),
             pltpu.VMEM((4, 64, HD), F32),
             pltpu.VMEM((64, HD), F32),
             pltpu.VMEM((64, HD), F32),
             dma((6,)),
             dma((4,)),
-            dma((6,)),
             dma((6,)),
             dma((6,)),
             dma((4,)),

time: 84.3 us -> 74.9 us (0.89)
  Pallas kernels: 83 us -> 73.2 us
    pallas_call x1, Pallas kernels: 80.4 us -> 70.7 us  [shards(): pl.pallas_call(step_kernel, out_shape=[pltpu.VMEM(shape, dtype) for shape...]
where the time goes in v2:
time: 74.9 us; the launch traced here: 74.5 us
  Pallas kernels  73.2 us (98%)
  between operations  1.29 us (2%)
    pallas_call x1, Pallas kernels, shards(): pl.pallas_call(step_kernel, out_shape=[pltpu.VMEM(shape, dtype) for shape...  70.7 us
    pallas_call x1, Pallas kernels, shards(): pl.pallas_call(finish_kernel, out_shape=[pltpu.HBM(shape, dtype) for shap...  2.54 us

profile of v2, /device:TPU:1, one launch (start us, length us, event | category | flops | bytes accessed | tf_op | source)
XLA Modules:
  0.0 74.5 jit_solution(4414825124758004956)
XLA Ops:
  1.3 70.7 %shard_map.135 = (bf16[128,1024]{1,0:T(8,128)(2,1)S(1)}, bf16[128,8192]{1,0:T(8,128)(2,1)S(1)}, f32[256,1024]{1,0:T(8,128)S(1)}, f32[256,1024]{1,0:T(8,128)S(1)}...) custom-call(s32[1]{0:T(128)S(6)} %copy.15.frag, bf16[128,8192]{1,0:T(8,128)(2,1)} %bitcast.10, ...), custom_call_target="tpu_custom_call" | custom-call | tf_op jit(solution)/shard_map/pallas_call | solution.py:450
  72.0 2.5 %shard_map.136 = (bf16[128,1024]{1,0:T(8,128)(2,1)}, bf16[128,8192]{1,0:T(8,128)(2,1)}, f32[256,1024]{1,0:T(8,128)}, f32[256,1024]{1,0:T(8,128)}, f32[256,1024]{...) custom-call(bf16[128,1024]{1,0:T(8,128)(2,1)S(1)} %get-tuple-element.21.refs_0_, ...), custom_call_target="tpu_custom_call" | custom-call | tf_op jit(solution)/shard_map/pallas_call | solution.py:519

commit v3 on v2

--- a/solution.py
+++ b/solution.py
@@ -81,6 +81,19 @@
     def own_rows(index):
         return pl.ds(pl.multiple_of(index * TOK, TOK), TOK)
 
+    barrier = pltpu.get_barrier_semaphore()
+
+    def greet(device):
+        pl.semaphore_signal(barrier, inc=1, device_id=device, device_id_type=MESH)
+
+    for i in range(1, 8):
+        gx, gc = group(i)
+        greet(at(gx, z, gc))
+    greet(at(x, p, c))
+    pl.when(inner == 1)(lambda: greet(at(x, q, c)))
+    for i in range(1, 4):
+        greet(rep_at((y + i) % 4, zh))
+
     load_w = pltpu.make_async_copy(w_in, wv, load_sem.at[0])
     load_of = pltpu.make_async_copy(of_in, ofv, load_sem.at[1])
     load_c = pltpu.make_async_copy(c_in, cots.at[own_rows(t), :], load_sem.at[2])
@@ -89,26 +102,11 @@
     load_v = pltpu.make_async_copy(v_in, vv, load_sem.at[5])
     for load in (load_w, load_of, load_c, load_om, load_m, load_v):
         load.start()
-    own_acts = []
     for b in range(4):
         load = pltpu.make_async_copy(
             a_in.at[:, pl.ds(column(x, b, c), 256)], acts.at[own_rows(t), block(b)], own_sem.at[b]
         )
         load.start()
-        own_acts.append(load)
-
-    barrier = pltpu.get_barrier_semaphore()
-
-    def greet(device):
-        pl.semaphore_signal(barrier, inc=1, device_id=device, device_id_type=MESH)
-
-    for i in range(1, 8):
-        gx, gc = group(i)
-        greet(at(gx, z, gc))
-    greet(at(x, p, c))
-    pl.when(inner == 1)(lambda: greet(at(x, q, c)))
-    for i in range(1, 4):
-        greet(rep_at((y + i) % 4, zh))
 
     load_w.wait()
     wall[block(z), :] = wv[...].astype(BF16)
@@ -140,12 +138,15 @@
     def half(index, side):
         return pl.ds(pl.multiple_of(index * TOK + side * 64, 64), 64)
 
+    load_c.wait()
+    mine = cots.at[own_rows(t), :]
+
     for slot, device in ((0, at(right, z, c)), (1, at(left, z, c))):
-        remote(c_in, cots.at[own_rows(t), :], c_send.at[slot], c_recv.at[slot], device).start()
-    remote(c_in, cots.at[own_rows(t), :], cf_send.at[0], cf_recv.at[0], at(x, z, 1 - c)).start()
-
-    def send_acts(b):
-        @pl.loop(1, 8)
+        remote(mine, mine, c_send.at[slot], c_recv.at[slot], device).start()
+    remote(mine, mine, cf_send.at[0], cf_recv.at[0], at(x, z, 1 - c)).start()
+
+    def send_acts(b, first=1, last=8):
+        @pl.loop(first, last)
         def _(i):
             gx, gc = group(i)
             remote(
@@ -153,7 +154,7 @@
                 a_send.at[0], a_recv.at[b], at(gx, z, gc),
             ).start()
 
-    send_acts(order[0])
+    send_acts(order[0], 3, 6)
 
     def chunk(index):
         return pl.ds(pl.multiple_of(index * 64, 64), 64)
@@ -172,6 +173,8 @@
         remote(
             cots.at[rows, :], cots.at[rows, :], cf_send.at[1 + slot], cf_recv.at[1 + slot], at(x, z, 1 - c)
         ).start()
+    send_acts(order[0], 1, 3)
+    send_acts(order[0], 6, 8)
     send_acts(order[1])
 
     @pl.when(inner == 1)
@@ -208,7 +211,6 @@
         wait_bytes(cots.at[half(far * 2 + c, slot), :], c_recv.at[2 + slot])
     rows = own_rows(far * 2 + c)
     remote(cots.at[rows, :], cots.at[rows, :], cf_send.at[3], cf_recv.at[3], at(x, z, 1 - c)).start()
-    load_c.wait()
     for slot, source in enumerate((x, left, right, far)):
         wait_bytes(cots.at[own_rows(source * 2 + 1 - c), :], cf_recv.at[slot])
 

time: 74.9 us -> 74.7 us (level)
  no operation moved by 1% of the time
where the time goes in v3:
time: 74.7 us; the launch traced here: 74.3 us
  Pallas kernels  73 us (98%)
  between operations  1.29 us (2%)
    pallas_call x1, Pallas kernels, shards(): pl.pallas_call(step_kernel, out_shape=[pltpu.VMEM(shape, dtype) for shape...  70.4 us
    pallas_call x1, Pallas kernels, shards(): pl.pallas_call(finish_kernel, out_shape=[pltpu.HBM(shape, dtype) for shap...  2.54 us

profile of v3, /device:TPU:1, one launch (start us, length us, event | category | flops | bytes accessed | tf_op | source)
XLA Modules:
  0.0 74.3 jit_solution(15967791182150969686)
XLA Ops:
  1.3 70.4 %shard_map.135 = (bf16[128,1024]{1,0:T(8,128)(2,1)S(1)}, bf16[128,8192]{1,0:T(8,128)(2,1)S(1)}, f32[256,1024]{1,0:T(8,128)S(1)}, f32[256,1024]{1,0:T(8,128)S(1)}...) custom-call(s32[1]{0:T(128)S(6)} %copy.15.frag, bf16[128,8192]{1,0:T(8,128)(2,1)} %bitcast.10, ...), custom_call_target="tpu_custom_call" | custom-call | tf_op jit(solution)/shard_map/pallas_call | solution.py:452
  71.7 2.5 %shard_map.136 = (bf16[128,1024]{1,0:T(8,128)(2,1)}, bf16[128,8192]{1,0:T(8,128)(2,1)}, f32[256,1024]{1,0:T(8,128)}, f32[256,1024]{1,0:T(8,128)}, f32[256,1024]{...) custom-call(bf16[128,1024]{1,0:T(8,128)(2,1)S(1)} %get-tuple-element.21.refs_0_, ...), custom_call_target="tpu_custom_call" | custom-call | tf_op jit(solution)/shard_map/pallas_call | solution.py:521
